TPU v7x, 32 devices: a whole 2x2x4 slice. The times are simulated.
32 devices in a mesh: events: 4 (over z), nodes: 8 (over y, x, core).
Axes of the slice: x: 2, y: 2, z: 4, core: 2. Of those that a mesh axis runs over, the one named last changes fastest.
Arguments:
- nodes_in: bfloat16 [4, 16384, 128], P('events', 'nodes'), may hold values from -6 to 6
- edge_latents: bfloat16 [4, 8, 8, 2, 128, 128], P('events', 'nodes'), may hold values from -6 to 6
- src_block: int32 [4, 8, 8, 2], P('events', 'nodes'), may hold values from 0 to 15
- src_offset: int32 [4, 8, 8, 2, 128], P('events', 'nodes'), may hold values from 0 to 127
- dst_block: int32 [4, 8, 8, 2], P('events', 'nodes'), may hold values from 0 to 15
- dst_offset: int32 [4, 8, 8, 2, 128], P('events', 'nodes'), may hold values from 0 to 127
- tile_counts: int32 [4, 8, 8], P('events'), may hold values from 1 to 2, as said below
- w_edge1: bfloat16 [384, 128], replicated, may hold values from -0.3125 to 0.3125
- b_edge1: float32 [128], replicated, may hold values from -3 to 3
- w_edge2: bfloat16 [128, 128], replicated, may hold values from -0.5 to 0.5
- b_edge2: float32 [128], replicated, may hold values from -3 to 3
- w_node1: bfloat16 [256, 128], replicated, may hold values from -0.375 to 0.375
- b_node1: float32 [128], replicated, may hold values from -3 to 3
- w_node2: bfloat16 [128, 128], replicated, may hold values from -0.5 to 0.5
- b_node2: float32 [128], replicated, may hold values from -3 to 3
- cotangent: bfloat16 [4, 16384, 128], P('events', 'nodes'), may hold values from -6 to 6
Outputs:
- new_nodes: bfloat16 [4, 16384, 128], P('events', 'nodes')
- node_grads: bfloat16 [4, 16384, 128], P('events', 'nodes')
- grad_w_edge1: float32 [384, 128], replicated
- grad_b_edge1: float32 [128], replicated
- grad_w_edge2: float32 [128, 128], replicated
- grad_b_edge2: float32 [128], replicated
- grad_w_node1: float32 [256, 128], replicated
- grad_b_node1: float32 [128], replicated
- grad_w_node2: float32 [128, 128], replicated
- grad_b_node2: float32 [128], replicated
Inputs may be any that keep to these rules, and one draw needn't show every extreme that they name: tile_counts[g, s, d] is the number of live slots from source device s to destination device d; in every event group some destination device receives exactly 2 tiles from every source device.
All inputs are finite; a program needn't handle non-finite values.
Results may differ from a plain program's by a relative error of at most 0.0067.
Values may be sent and summed in bfloat16 or wider, within the bound.
A program may use at most 64 MiB of HBM per device.

v0:
```python
import jax
import jax.numpy as jnp
from jax import lax
from jax.sharding import PartitionSpec as P


def silu_slope(value):
    sig = jax.nn.sigmoid(value)
    return sig * (1.0 + value * (1.0 - sig))


def tile_onehot(offsets, tile):
    return (offsets[..., None] == jnp.arange(tile, dtype=jnp.int32)[None, None, :]).astype(
        jnp.bfloat16
    )


def gather_tiles(table, blocks, onehot):
    tile = onehot.shape[-1]
    picked = table.reshape(-1, tile, table.shape[-1])[blocks]
    return jnp.einsum("ten,tnd->ted", onehot, picked, preferred_element_type=jnp.float32).astype(
        table.dtype
    )


def scatter_tiles(values, blocks, onehot, block_count):
    if values.dtype == jnp.bfloat16:
        per_tile = jnp.einsum("ten,ted->tnd", onehot, values, preferred_element_type=jnp.float32)
    else:
        per_tile = jnp.einsum(
            "ten,ted->tnd", onehot.astype(jnp.float32), values, precision=lax.Precision.HIGHEST
        )
    picker = (blocks[:, None] == jnp.arange(block_count, dtype=jnp.int32)[None, :]).astype(
        jnp.float32
    )
    summed = jnp.einsum("tb,tnd->bnd", picker, per_tile, precision=lax.Precision.HIGHEST)
    return summed.reshape(-1, values.shape[-1])


def shards(
    nodes_in,
    edge_latents,
    src_block,
    src_offset,
    dst_block,
    dst_offset,
    tile_counts,
    w_edge1,
    b_edge1,
    w_edge2,
    b_edge2,
    w_node1,
    b_node1,
    w_node2,
    b_node2,
    cotangent,
):
    peers = lax.axis_size("nodes")
    myself = lax.axis_index("nodes")
    nodes = nodes_in[0]
    cot = cotangent[0]
    node_rows, width = nodes.shape
    tile = src_offset.shape[-1]
    slots = src_offset.shape[3]
    block_count = node_rows // tile
    tiles_all = peers * slots
    scale_factor = float(lax.axis_size("events") * peers * node_rows) ** (-0.5)
    w_src, w_dst, w_lat = (w_edge1[:width], w_edge1[width : 2 * width], w_edge1[2 * width :])
    w_own, w_agg = (w_node1[:width], w_node1[width:])
    send_blocks = src_block[0, 0].reshape(-1)
    send_hot = tile_onehot(src_offset[0, 0].reshape(tiles_all, tile), tile)
    recv_blocks = dst_block[0, 0].reshape(-1)
    recv_hot = tile_onehot(dst_offset[0, 0].reshape(tiles_all, tile), tile)
    outgoing = gather_tiles(nodes, send_blocks, send_hot).reshape(peers, slots, tile, width)
    h_src = lax.all_to_all(outgoing, "nodes", split_axis=0, concat_axis=0, tiled=True).reshape(
        -1, width
    )
    counts = lax.dynamic_index_in_dim(tile_counts[0], myself, 1, keepdims=False)
    live = jnp.arange(slots, dtype=jnp.int32)[None, :] < counts[:, None]
    live = (
        jnp.broadcast_to(live[..., None], (peers, slots, tile)).reshape(-1, 1).astype(jnp.bfloat16)
    )
    lat = edge_latents[0, 0].reshape(-1, width)
    h_dst = gather_tiles(nodes, recv_blocks, recv_hot).reshape(-1, width)
    z_one = (
        jnp.dot(h_src, w_src, preferred_element_type=jnp.float32)
        + jnp.dot(h_dst, w_dst, preferred_element_type=jnp.float32)
        + jnp.dot(lat, w_lat, preferred_element_type=jnp.float32)
        + b_edge1
    )
    a_one = jax.nn.silu(z_one).astype(jnp.bfloat16)
    message = (jnp.dot(a_one, w_edge2, preferred_element_type=jnp.float32) + b_edge2).astype(
        jnp.bfloat16
    ) * live
    agg = scatter_tiles(
        message.reshape(tiles_all, tile, width), recv_blocks, recv_hot, block_count
    ).astype(jnp.bfloat16)
    z_two = (
        jnp.dot(nodes, w_own, preferred_element_type=jnp.float32)
        + jnp.dot(agg, w_agg, preferred_element_type=jnp.float32)
        + b_node1
    )
    a_two = jax.nn.silu(z_two).astype(jnp.bfloat16)
    updated = (
        nodes.astype(jnp.float32)
        + jnp.dot(a_two, w_node2, preferred_element_type=jnp.float32)
        + b_node2
    ).astype(jnp.bfloat16)
    g_two = (
        jnp.dot(cot, w_node2.T, preferred_element_type=jnp.float32) * silu_slope(z_two)
    ).astype(jnp.bfloat16)
    node_terms = (
        jnp.concatenate(
            [
                jnp.dot(nodes.T, g_two, preferred_element_type=jnp.float32),
                jnp.dot(agg.T, g_two, preferred_element_type=jnp.float32),
            ],
            axis=0,
        ),
        jnp.sum(g_two.astype(jnp.float32), axis=0),
        jnp.dot(a_two.T, cot, preferred_element_type=jnp.float32),
        jnp.sum(cot.astype(jnp.float32), axis=0),
    )
    g_agg = jnp.dot(g_two, w_agg.T, preferred_element_type=jnp.float32).astype(jnp.bfloat16)
    g_msg = gather_tiles(g_agg, recv_blocks, recv_hot).reshape(-1, width) * live
    g_one = (
        jnp.dot(g_msg, w_edge2.T, preferred_element_type=jnp.float32) * silu_slope(z_one)
    ).astype(jnp.bfloat16)
    g_src = jnp.dot(g_one, w_src.T, preferred_element_type=jnp.float32).reshape(
        peers, slots, tile, width
    )
    returned = (
        lax.all_to_all(g_src.astype(jnp.bfloat16), "nodes", split_axis=0, concat_axis=0, tiled=True)
        .astype(g_src.dtype)
        .reshape(-1, width)
    )
    g_dst = jnp.dot(g_one, w_dst.T, preferred_element_type=jnp.float32)
    total = cot.astype(jnp.float32) + jnp.dot(g_two, w_own.T, preferred_element_type=jnp.float32)
    total = total + scatter_tiles(
        g_dst.reshape(tiles_all, tile, width), recv_blocks, recv_hot, block_count
    )
    total = total + scatter_tiles(
        returned.reshape(tiles_all, tile, width), send_blocks, send_hot, block_count
    )
    edge_terms = (
        jnp.concatenate(
            [
                jnp.dot(h_src.T, g_one, preferred_element_type=jnp.float32),
                jnp.dot(h_dst.T, g_one, preferred_element_type=jnp.float32),
                jnp.dot(lat.T, g_one, preferred_element_type=jnp.float32),
            ],
            axis=0,
        ),
        jnp.sum(g_one.astype(jnp.float32), axis=0),
        jnp.dot(a_one.T, g_msg, preferred_element_type=jnp.float32),
        jnp.sum(g_msg.astype(jnp.float32), axis=0),
    )
    summed = lax.psum(
        (
            edge_terms[0],
            edge_terms[1],
            edge_terms[2],
            edge_terms[3],
            node_terms[0],
            node_terms[1],
            node_terms[2],
            node_terms[3],
        ),
        ("events", "nodes"),
    )
    scaled = [value * scale_factor for value in summed]
    return (
        updated[None],
        total.astype(jnp.bfloat16)[None],
        scaled[0],
        scaled[1],
        scaled[2],
        scaled[3],
        scaled[4],
        scaled[5],
        scaled[6],
        scaled[7],
    )


def solution(mesh):
    return jax.shard_map(
        shards,
        mesh=mesh,
        in_specs=(
            P("events", "nodes", None),
            P("events", "nodes", None, None, None, None),
            P("events", "nodes", None, None),
            P("events", "nodes", None, None, None),
            P("events", "nodes", None, None),
            P("events", "nodes", None, None, None),
            P("events", None, None),
            P(),
            P(),
            P(),
            P(),
            P(),
            P(),
            P(),
            P(),
            P("events", "nodes", None),
        ),
        out_specs=(
            P("events", "nodes", None),
            P("events", "nodes", None),
            P(),
            P(),
            P(),
            P(),
            P(),
            P(),
            P(),
            P(),
        ),
        check_vma=False,
    )
```

profile of v0, /device:TPU:0, one launch (start us, length us, event | category | flops | bytes accessed | tf_op | source)
XLA Modules:
  0.0 243.3 jit_solution(3081769146235548526)
XLA Ops:
  7.2 0.8 copy.33
  8.1 1.7 gather_fusion
  9.8 1.3 convolution_convert_fusion.4
  11.1 5.3 %all-to-all-start = ((bf16[8,2,128,128]{3,2,1,0:T(8,128)(2,1)}), bf16[8,2,128,128]{3,2,1,0:T(8,128)(2,1)S(1)}, u32[]{:S(2)}, u32[]{:S(2)}) async-start(bf16[8,2,128,128]{3,2,1,0:T(8,128)(2,1)} %bitcast.6), calls=%async_computation | async-start | bytes 1048576 | tf_op jit(solution)/shard_map/all_to_all | solution.py:75
  20.0 0.9 convert_reduce_fusion
  20.9 1.2 fusion.25
  22.1 4.0 %all-to-all-done = bf16[8,2,128,128]{3,2,1,0:T(8,128)(2,1)S(1)} async-done(((bf16[8,2,128,128]{3,2,1,0:T(8,128)(2,1)}), bf16[8,2,128,128]{3,2,1,0:T(8,128)(2,1)S(1)}, u32[]{:S(2)}, u32[]{:S(2)}) %all-to-all-start) | async-done | bytes 524320 | tf_op jit(solution)/shard_map/all_to_all | solution.py:75
  27.4 1.4 multiply_convert_fusion.1
  29.9 1.0 fusion.20
  30.9 1.2 convolution_convert_fusion.5
  33.0 1.2 multiply_convert_fusion
  34.2 1.0 convert_reduce_fusion.1
  35.9 1.1 convolution_convert_fusion.1
  37.0 2.5 %gather_fusion.2 = bf16[16,128,128]{2,1,0:T(8,128)(2,1)} fusion(bf16[16,128,128]{2,1,0:T(8,128)(2,1)} %bitcast.107, s32[1024]{0:T(1024)S(1)} %pad_clamp_fusion), kind=kCustom, calls=%fused_computation.2 | custom fusion | bytes 1048640 | tf_op jit(solution)/shard_map/gather | solution.py:20
  39.5 2.3 convert_reduce_fusion.2
  42.1 0.7 copy-done.6
  42.8 1.0 fusion.57
  43.7 1.0 convert_reduce_fusion.3
  46.3 1.1 convolution_convert_fusion
  47.8 0.7 copy-done.3
  48.5 1.0 fusion.21
  49.5 1.1 fusion.11
  50.5 4.1 %all-to-all-start.1 = ((bf16[8,2,128,128]{3,2,1,0:T(8,128)(2,1)}), bf16[8,2,128,128]{3,2,1,0:T(8,128)(2,1)}, u32[]{:S(2)}, u32[]{:S(2)}) async-start(bf16[8,2,128,128]{3,2,1,0:T(8,128)(2,1)} %bitcast.104), calls=%async_computation.1 | async-start | bytes 1048576 | tf_op jit(solution)/shard_map/all_to_all | solution.py:133
  54.9 1.5 fusion.19
  56.5 2.2 fusion.15
  60.7 40.6 %all-reduce = (f32[128]{0:T(128)S(1)}, f32[128]{0:T(128)S(1)}, f32[128]{0:T(128)S(1)}, f32[128]{0:T(128)S(1)}) all-reduce(f32[128]{0:T(128)S(1)} %copy-done.26, f32[128]{0:T(128)S(1)} %copy-done.25, f32[128]{0:T(128)S(1)} %copy-done.24, f32[128]{0:T(128)S(1)} %copy-done.21), channel_id=1, replica_groups=mesh['events'=4,'nodes'=8] {'events','nodes'}, use_global_device_ids=true, to_apply=%region_2.3 | all-reduce | flops 512 | bytes 4096 | tf_op jit(solution)/shard_map/psum | solution.py:158
  101.8 1.6 copy.36
  103.9 124.8 %all-reduce.4.cloned.1.call-done = (f32[384,128]{1,0:T(8,128)}, f32[128,128]{1,0:T(8,128)}, f32[256,128]{1,0:T(8,128)}, f32[128,128]{1,0:T(8,128)}) async-done(((f32[384,128]{1,0:T(8,128)}, f32[128,128]{1,0:T(8,128)}, f32[256,128]{1,0:T(8,128)}, f32[128,128]{1,0:T(8,128)}), (f32[384,128]{1,0:T(8,128)}, f32[128,128]{1,0:T(8,128)}, f32[256,128]{1,0:T(8,128)}, ...) | async-done | bytes 458768 | tf_op jit(solution)/shard_map/psum | solution.py:158
  228.7 1.6 broadcast_multiply_fusion.1
  232.0 1.8 fusion.18
  233.8 1.2 fusion.13
  235.3 1.1 fusion.10
  (98 shorter events, 15.0 us)
Async XLA Ops:
  7.2 19.5 %copy-start = (bf16[1,1,8,2,128,128]{5,4,3,2,1,0:T(8,128)(2,1)S(1)}, bf16[1,1,8,2,128,128]{5,4,3,2,1,0:T(8,128)(2,1)}, u32[]{:S(2)}) copy-start(bf16[1,1,8,2,128,128]{5,4,3,2,1,0:T(8,128)(2,1)} %param.17) | copy-start | bytes 1572868
  8.1 1.7 copy-start.14
  11.1 6.2 %copy-start.1 = (bf16[1,2048,128]{2,1,0:T(8,128)(2,1)S(1)}, bf16[1,2048,128]{2,1,0:T(8,128)(2,1)}, u32[]{:S(2)}) copy-start(bf16[1,2048,128]{2,1,0:T(8,128)(2,1)} %param.16) | copy-start | bytes 1572868
  11.1 15.0 %all-to-all-start = ((bf16[8,2,128,128]{3,2,1,0:T(8,128)(2,1)}), bf16[8,2,128,128]{3,2,1,0:T(8,128)(2,1)S(1)}, u32[]{:S(2)}, u32[]{:S(2)}) async-start(bf16[8,2,128,128]{3,2,1,0:T(8,128)(2,1)} %bitcast.6), calls=%async_computation | async-start | bytes 1048576 | tf_op jit(solution)/shard_map/all_to_all | solution.py:75
  16.4 0.7 copy-start.22
  17.3 0.7 copy-start.19
  17.9 0.7 copy-start.11
  18.6 1.4 copy-start.2
  19.9 11.0 %copy-start.17 = (s32[16]{0:T(128)}, s32[16]{0:T(128)S(1)}, u32[]{:S(2)}) copy-start(s32[16]{0:T(128)S(1)} %eq.32) | copy-start | bytes 196
  20.0 0.9 copy-start.10
  20.9 5.2 %copy-start.8 = (bf16[384,128]{1,0:T(8,128)(2,1)S(1)}, bf16[384,128]{1,0:T(8,128)(2,1)}, u32[]{:S(2)}) copy-start(bf16[384,128]{1,0:T(8,128)(2,1)} %param.23) | copy-start | bytes 294916
  27.4 1.5 copy-start.27
  28.8 1.1 copy-start.5
  28.9 0.7 copy-start.29
  30.9 1.4 copy-start.4
  33.0 1.3 copy-start.15
  41.7 1.0 copy-start.6
  41.7 2.0 copy-start.31
  45.5 0.9 copy-start.9
  47.4 1.0 copy-start.3
  48.5 1.0 copy-start.16
  48.5 1.0 copy-start.23
  50.5 181.4 %all-to-all-start.1 = ((bf16[8,2,128,128]{3,2,1,0:T(8,128)(2,1)}), bf16[8,2,128,128]{3,2,1,0:T(8,128)(2,1)}, u32[]{:S(2)}, u32[]{:S(2)}) async-start(bf16[8,2,128,128]{3,2,1,0:T(8,128)(2,1)} %bitcast.104), calls=%async_computation.1 | async-start | bytes 1048576 | tf_op jit(solution)/shard_map/all_to_all | solution.py:133
  54.7 174.0 %all-reduce.4.cloned.1.call-start = ((), (), s32[]{:S(2)}) async-start(), calls=%async_computation.2 | async-start | bytes 917504 | tf_op jit(solution)/shard_map/psum | solution.py:158
  54.9 1.5 copy-start.18
  59.4 0.7 copy-start.26
  60.0 0.7 copy-start.24
  60.1 0.7 copy-start.25
  228.7 1.6 copy-start.12
  228.7 1.6 copy-start.13
  230.3 1.0 copy-start.7
  232.0 1.8 copy-start.20
  (3 other events, 2.0 us)
Sparse Core Ops, SparseCore 0:
  101.4 127.2 all-reduce.3
where the time goes:
time: 245 us; the launch traced here: 243 us
  waiting for transfers between devices  129 us (53%)
  blocking collectives  40.6 us (17%)
  matrix products  28.1 us (11%)
  local copies, waits for them, and re-layouts  15.2 us (6%)
  between operations  14.4 us (6%)
  starting transfers between devices  9.67 us (4%)
  other arithmetic  6.65 us (3%)
    psum x1, waiting for transfers between devices, shards(): lax.psum((edge_terms[0], edge_terms[1], edge_terms[2], edge_terms[3], nod...  125 us
    psum x1, blocking collectives, shards(): lax.psum((edge_terms[0], edge_terms[1], edge_terms[2], edge_terms[3], nod...  40.6 us
    unnamed x66, local copies, waits for them, and re-layouts  7.09 us
    all_to_all x1, starting transfers between devices, shards(): lax.all_to_all(outgoing, 'nodes', split_axis=0, concat_axis=0, tiled=True)  5.3 us
  transfers between devices with their start and end apart: 3, of which 2 were waited for; matrix products, arithmetic and copies ran while one was open for 6% of the time, Pallas kernels for 0%

commit v1 on v0

v1 whole, which is shorter than its diff:
```python
import functools

import jax
import jax.numpy as jnp
from jax import lax
from jax.experimental import pallas as pl
from jax.experimental.pallas import tpu as pltpu
from jax.sharding import PartitionSpec as P

F32 = jnp.float32
BF16 = jnp.bfloat16
MESH = pl.DeviceIdType.MESH


def dot(a, b):
    return jnp.dot(a, b, preferred_element_type=F32)


def dot_tl(a, b):
    return lax.dot_general(a, b, (((0,), (0,)), ((), ())), preferred_element_type=F32)


def dot_tr(a, b):
    return lax.dot_general(a, b, (((1,), (1,)), ((), ())), preferred_element_type=F32)


def act(v):
    s = jax.nn.sigmoid(v)
    return v * s, s * (1.0 + v * (1.0 - s))


def kernel(
    peers,
    zs,
    scale,
    nodes,
    lat,
    sblk,
    soff,
    dblk,
    doff,
    cnt,
    w1,
    b1,
    w2,
    b2,
    wn1,
    bn1,
    wn2,
    bn2,
    cot,
    upd,
    ngrad,
    gw1,
    gb1,
    gw2,
    gb2,
    gwn1,
    gbn1,
    gwn2,
    gbn2,
    hs,
    rh,
    ps,
    pd,
    hd,
    slope,
    a1,
    gm,
    g1,
    ret,
    st,
    st2,
    cw,
    agg,
    a2,
    g2,
    gag,
    sd,
    red,
    rbuf,
    zbuf,
    abuf,
    s_a,
    r_a,
    s_b,
    r_b,
    s_r,
    r_r,
    s_z,
    r_z,
    s_g,
    r_g,
):
    me = lax.axis_index("nodes")
    mz = lax.axis_index("events")
    slots, tile = soff.shape[3], soff.shape[4]
    nblk, width = nodes.shape[1], nodes.shape[3]
    rows = nblk * tile
    chunk = rbuf.shape[1]
    pair = slots * tile

    barrier = pltpu.get_barrier_semaphore()

    def greet(axis, mine, size):
        def body(i, c):
            pl.semaphore_signal(
                barrier, 1, device_id={axis: lax.rem(mine + i, size)}, device_id_type=MESH
            )
            return c

        lax.fori_loop(1, size, body, 0)

    greet("nodes", me, peers)
    greet("events", mz, zs)

    iota = lax.broadcasted_iota(jnp.int32, (tile, tile), 0)

    def onehot(off):
        return jnp.where(iota == off, 1.0, 0.0).astype(BF16)

    def copy(src, dst, s_sem, r_sem, axis, to):
        return pltpu.make_async_remote_copy(
            src_ref=src,
            dst_ref=dst,
            send_sem=s_sem,
            recv_sem=r_sem,
            device_id={axis: to},
            device_id_type=MESH,
        )

    def gather_src(p, into):
        for k in range(slots):
            hot = onehot(soff[0, 0, p, k : k + 1, :])
            ps[p, k] = hot
            block = nodes[0, sblk[0, 0, p, k]]
            into[p, k] = dot_tl(hot, block).astype(BF16)

    gather_src(me, rh)
    pl.semaphore_wait(barrier, peers - 1 + zs - 1)

    def copy_a(p):
        return copy(hs.at[p], rh.at[me], s_a.at[p], r_a.at[me], "nodes", p)

    def send_a(i, c):
        p = lax.rem(me + i, peers)
        gather_src(p, hs)
        copy_a(p).start()
        return c

    lax.fori_loop(1, peers, send_a, 0)

    def local(s, c):
        h = []
        for k in range(slots):
            live = jnp.minimum(jnp.maximum(cnt[0, s, me] - k, 0), 1)
            hot = onehot(doff[0, 0, s, k : k + 1, :] * live + (live - 1))
            pd[s, k] = hot
            block = nodes[0, dblk[0, 0, s, k]]
            h.append(dot_tl(hot, block).astype(BF16))
            hd[s, k] = h[k]
        x = jnp.concatenate(
            [jnp.concatenate(h, axis=0), lat[0, 0, s].reshape(pair, width)], axis=1
        )
        z = dot(x, w1[width:, :]) + b1[...]
        slope[s] = z.reshape(slots, tile, width)
        return c

    lax.fori_loop(0, peers, local, 0)

    cw[...] = dot_tr(cot[0], wn2[...])

    def forward(s):
        z = slope[s].reshape(pair, width) + dot(rh[s].reshape(pair, width), w1[:width, :])
        a, d = act(z)
        a = a.astype(BF16)
        slope[s] = d.reshape(slots, tile, width)
        a1[s] = a.reshape(slots, tile, width)
        msg = (dot(a, w2[...]) + b2[...]).astype(BF16)
        for k in range(slots):
            st[s, k] = dot(pd[s, k], msg[k * tile : (k + 1) * tile])

    forward(me)

    def recv_a(i, c):
        s = lax.rem(me + peers - i, peers)
        copy(hs.at[s], rh.at[s], s_a.at[s], r_a.at[s], "nodes", s).wait_recv()
        forward(s)
        return c

    lax.fori_loop(1, peers, recv_a, 0)

    def spread(parts, blocks, b):
        def body(s, acc):
            for k in range(slots):
                gap = blocks[0, 0, s, k] - b
                acc = acc + (1 - jnp.minimum(gap * gap, 1)).astype(F32) * parts[s, k]
            return acc

        return lax.fori_loop(
            0, peers, body, jnp.zeros((tile, width), F32), unroll=True if peers <= 8 else 8
        )

    group = 4 if nblk % 4 == 0 else 1
    span = group * tile

    def node(c, carry):
        at = pl.ds(pl.multiple_of(c * span, span), span)
        ag = jnp.concatenate(
            [spread(st, dblk, c * group + j).astype(BF16) for j in range(group)], axis=0
        )
        agg[at, :] = ag
        h = nodes[0, pl.ds(c * group, group)].reshape(span, width)
        z = dot(jnp.concatenate([h, ag], axis=1), wn1[...]) + bn1[...]
        a, d = act(z)
        a = a.astype(BF16)
        a2[at, :] = a
        upd[0, at, :] = (h.astype(F32) + dot(a, wn2[...]) + bn2[...]).astype(BF16)
        g = (cw[at, :] * d).astype(BF16)
        g2[at, :] = g
        gag[pl.ds(c * group, group)] = (
            dot_tr(g, wn1[width:, :]).astype(BF16).reshape(group, tile, width)
        )
        return carry

    lax.fori_loop(0, nblk // group, node, 0)

    def back(s):
        g = []
        for k in range(slots):
            block = gag[dblk[0, 0, s, k]]
            g.append(dot_tl(pd[s, k], block).astype(BF16))
            gm[s, k] = g[k]
        one = dot_tr(jnp.concatenate(g, axis=0), w2[...]) * slope[s].reshape(pair, width)
        return one.astype(BF16).reshape(slots, tile, width)

    def copy_b(p):
        return copy(g1.at[p], ret.at[me], s_b.at[p], r_b.at[me], "nodes", p)

    def send_b(i, c):
        p = lax.rem(me + i, peers)
        g1[p] = back(p)
        copy_b(p).start()
        return c

    lax.fori_loop(1, peers, send_b, 0)
    own = back(me)
    g1[me] = own
    ret[me] = own

    per = 8 if peers % 8 == 0 else peers
    span_e = per * pair

    def edges(c, carry):
        e1, e2, s1, s2 = carry
        at = pl.ds(c * per, per)
        g = g1[at].reshape(span_e, width)
        x = jnp.concatenate(
            [
                rh[at].reshape(span_e, width),
                hd[at].reshape(span_e, width),
                lat[0, 0, at].reshape(span_e, width),
            ],
            axis=1,
        )
        m = gm[at].reshape(span_e, width)
        e1 = e1 + dot_tl(g, x)
        e2 = e2 + dot_tl(a1[at].reshape(span_e, width), m)
        s1 = s1 + jnp.sum(g.astype(F32), axis=0, keepdims=True)
        s2 = s2 + jnp.sum(m.astype(F32), axis=0, keepdims=True)
        return e1, e2, s1, s2

    zero = jnp.zeros((1, width), F32)
    e1, e2, s1, s2 = lax.fori_loop(
        0,
        peers // per,
        edges,
        (jnp.zeros((width, 3 * width), F32), jnp.zeros((width, width), F32), zero, zero),
    )
    for j in range(3):
        red[j * width : (j + 1) * width, :] = e1[:, j * width : (j + 1) * width].T.astype(BF16)
    red[3 * width : 4 * width, :] = e2.astype(BF16)
    g = g2[...]
    n1 = dot_tl(g, jnp.concatenate([nodes[0].reshape(rows, width), agg[...]], axis=1))
    for j in range(2):
        red[(4 + j) * width : (5 + j) * width, :] = n1[:, j * width : (j + 1) * width].T.astype(
            BF16
        )
    red[6 * width : 7 * width, :] = dot_tl(a2[...], cot[0]).astype(BF16)
    s3 = jnp.sum(g.astype(F32), axis=0, keepdims=True)
    s4 = jnp.sum(cot[0].astype(F32), axis=0, keepdims=True)
    rest = red.shape[0] - 7 * width
    line = lax.broadcasted_iota(jnp.int32, (rest, width), 0)
    tail = jnp.zeros((rest, width), F32)
    for j, s in enumerate((s1, s2, s3, s4)):
        tail = jnp.where(line == j, s, tail)
    red[7 * width :, :] = tail.astype(BF16)

    def part(p):
        return pl.ds(pl.multiple_of(p * chunk, chunk), chunk)

    def copy_r(p):
        return copy(red.at[part(p), :], rbuf.at[me], s_r.at[p], r_r.at[me], "nodes", p)

    def send_r(i, c):
        copy_r(lax.rem(me + i, peers)).start()
        return c

    lax.fori_loop(1, peers, send_r, 0)
    rbuf[me] = red[part(me), :]

    def tiles_d(s, c):
        for k in range(slots):
            st[s, k] = dot(pd[s, k], g1[s, k])
        return c

    lax.fori_loop(0, peers, tiles_d, 0)

    def spread_d(b, c):
        sd[pl.ds(pl.multiple_of(b * tile, tile), tile), :] = spread(st, dblk, b).astype(BF16)
        return c

    lax.fori_loop(0, nblk, spread_d, 0)

    def recv_r(i, c):
        s = lax.rem(me + i, peers)
        copy(red.at[part(s), :], rbuf.at[s], s_r.at[s], r_r.at[s], "nodes", s).wait_recv()
        return c

    lax.fori_loop(1, peers, recv_r, 0)
    zbuf[mz] = jnp.sum(rbuf[...].astype(F32), axis=0).astype(BF16)

    def copy_z(p):
        return copy(zbuf.at[mz], zbuf.at[mz], s_z.at[p], r_z.at[mz], "events", p)

    def send_z(i, c):
        copy_z(lax.rem(mz + i, zs)).start()
        return c

    lax.fori_loop(1, zs, send_z, 0)

    def tiles_s(s):
        for k in range(slots):
            st2[s, k] = dot(ps[s, k], ret[s, k])

    tiles_s(me)

    def recv_b(i, c):
        s = lax.rem(me + peers - i, peers)
        copy(g1.at[s], ret.at[s], s_b.at[s], r_b.at[s], "nodes", s).wait_recv()
        tiles_s(s)
        return c

    lax.fori_loop(1, peers, recv_b, 0)

    def recv_z(i, c):
        s = lax.rem(mz + i, zs)
        copy(zbuf.at[s], zbuf.at[s], s_z.at[s], r_z.at[s], "events", s).wait_recv()
        return c

    lax.fori_loop(1, zs, recv_z, 0)
    abuf[me] = (jnp.sum(zbuf[...].astype(F32), axis=0) * scale).astype(BF16)

    def copy_g(p):
        return copy(abuf.at[me], abuf.at[me], s_g.at[p], r_g.at[me], "nodes", p)

    def send_g(i, c):
        copy_g(lax.rem(me + i, peers)).start()
        return c

    lax.fori_loop(1, peers, send_g, 0)

    def final(c, carry):
        at = pl.ds(pl.multiple_of(c * span, span), span)
        ss = jnp.concatenate(
            [spread(st2, sblk, c * group + j).astype(BF16) for j in range(group)], axis=0
        )
        total = (
            cot[0, at, :].astype(F32)
            + dot_tr(g2[at, :], wn1[:width, :])
            + dot_tr(sd[at, :], w1[width : 2 * width, :])
            + dot_tr(ss, w1[:width, :])
        )
        ngrad[0, at, :] = total.astype(BF16)
        return carry

    lax.fori_loop(0, nblk // group, final, 0)

    def recv_g(i, c):
        s = lax.rem(me + i, peers)
        copy(abuf.at[s], abuf.at[s], s_g.at[s], r_g.at[s], "nodes", s).wait_recv()
        return c

    lax.fori_loop(1, peers, recv_g, 0)
    full = abuf[...].reshape(peers * chunk, width)
    gw1[...] = full[: 3 * width].astype(F32)
    gw2[...] = full[3 * width : 4 * width].astype(F32)
    gwn1[...] = full[4 * width : 6 * width].astype(F32)
    gwn2[...] = full[6 * width : 7 * width].astype(F32)
    last = full[7 * width : 7 * width + 16].astype(F32)
    gb1[...] = last[0:1]
    gb2[...] = last[1:2]
    gbn1[...] = last[2:3]
    gbn2[...] = last[3:4]

    def drain(i, c):
        p = lax.rem(me + i, peers)
        copy_a(p).wait_send()
        copy_b(p).wait_send()
        copy_r(p).wait_send()
        copy_g(p).wait_send()
        return c

    lax.fori_loop(1, peers, drain, 0)

    def drain_z(i, c):
        copy_z(lax.rem(mz + i, zs)).wait_send()
        return c

    lax.fori_loop(1, zs, drain_z, 0)


def shards(
    peers,
    zs,
    nodes_in,
    edge_latents,
    src_block,
    src_offset,
    dst_block,
    dst_offset,
    tile_counts,
    w_edge1,
    b_edge1,
    w_edge2,
    b_edge2,
    w_node1,
    b_node1,
    w_node2,
    b_node2,
    cotangent,
):
    rows, width = nodes_in.shape[1:]
    slots, tile = src_offset.shape[3:]
    scale = float(zs * peers * rows) ** (-0.5)
    need = 7 * width + 16
    chunk = -(-need // (16 * peers)) * 16
    vec = lambda v: v.reshape(1, -1)
    vm = pl.BlockSpec(memory_space=pltpu.VMEM)
    sm = pl.BlockSpec(memory_space=pltpu.SMEM)
    tiles = (peers, slots, tile, width)
    sds = jax.ShapeDtypeStruct
    dma = pltpu.SemaphoreType.DMA
    outs = pl.pallas_call(
        functools.partial(kernel, peers, zs, scale),
        out_shape=(
            sds((1, rows, width), BF16),
            sds((1, rows, width), BF16),
            sds((3 * width, width), F32),
            sds((1, width), F32),
            sds((width, width), F32),
            sds((1, width), F32),
            sds((2 * width, width), F32),
            sds((1, width), F32),
            sds((width, width), F32),
            sds((1, width), F32),
        ),
        in_specs=[vm, vm, sm, vm, sm, vm, sm] + [vm] * 9,
        out_specs=(vm,) * 10,
        scratch_shapes=[
            pltpu.VMEM(tiles, BF16),
            pltpu.VMEM(tiles, BF16),
            pltpu.VMEM((peers, slots, tile, tile), BF16),
            pltpu.VMEM((peers, slots, tile, tile), BF16),
            pltpu.VMEM(tiles, BF16),
            pltpu.VMEM(tiles, F32),
            pltpu.VMEM(tiles, BF16),
            pltpu.VMEM(tiles, BF16),
            pltpu.VMEM(tiles, BF16),
            pltpu.VMEM(tiles, BF16),
            pltpu.VMEM(tiles, F32),
            pltpu.VMEM(tiles, F32),
            pltpu.VMEM((rows, width), F32),
            pltpu.VMEM((rows, width), BF16),
            pltpu.VMEM((rows, width), BF16),
            pltpu.VMEM((rows, width), BF16),
            pltpu.VMEM((rows // tile, tile, width), BF16),
            pltpu.VMEM((rows, width), BF16),
            pltpu.VMEM((peers * chunk, width), BF16),
            pltpu.VMEM((peers, chunk, width), BF16),
            pltpu.VMEM((zs, chunk, width), BF16),
            pltpu.VMEM((peers, chunk, width), BF16),
        ]
        + [dma((peers,))] * 6
        + [dma((zs,))] * 2
        + [dma((peers,))] * 2,
        compiler_params=pltpu.CompilerParams(
            collective_id=0, has_side_effects=True, vmem_limit_bytes=48 * 1024 * 1024
        ),
    )(
        nodes_in.reshape(1, rows // tile, tile, width),
        edge_latents,
        src_block,
        src_offset,
        dst_block,
        dst_offset,
        tile_counts,
        w_edge1,
        vec(b_edge1),
        w_edge2,
        vec(b_edge2),
        w_node1,
        vec(b_node1),
        w_node2,
        vec(b_node2),
        cotangent,
    )
    outs = list(outs)
    for j in (3, 5, 7, 9):
        outs[j] = outs[j].reshape(-1)
    return tuple(outs)


def solution(mesh):
    return jax.shard_map(
        functools.partial(shards, mesh.shape["nodes"], mesh.shape["events"]),
        mesh=mesh,
        in_specs=(
            P("events", "nodes", None),
            P("events", "nodes", None, None, None, None),
            P("events", "nodes", None, None),
            P("events", "nodes", None, None, None),
            P("events", "nodes", None, None),
            P("events", "nodes", None, None, None),
            P("events", None, None),
            P(),
            P(),
            P(),
            P(),
            P(),
            P(),
            P(),
            P(),
            P("events", "nodes", None),
        ),
        out_specs=(
            P("events", "nodes", None),
            P("events", "nodes", None),
            P(),
            P(),
            P(),
            P(),
            P(),
            P(),
            P(),
            P(),
        ),
        check_vma=False,
    )
```

time: 245 us -> 53.6 us (0.22)
  waiting for transfers between devices: 129 us -> 0 us
  blocking collectives: 40.6 us -> 0 us
  Pallas kernels: 0 us -> 37.5 us
  matrix products: 28.1 us -> 0 us
  between operations: 14.4 us -> 0.73 us
  starting transfers between devices: 9.67 us -> 0 us
  other arithmetic: 6.65 us -> 0 us
    psum x1 -> x0, waiting for transfers between devices: 125 us -> none  [shards(): lax.psum((edge_terms[0], edge_terms[1], edge_terms[2], edge_terms[3], nod...]
    psum x1 -> x0, blocking collectives: 40.6 us -> none  [shards(): lax.psum((edge_terms[0], edge_terms[1], edge_terms[2], edge_terms[3], nod...]
    pallas_call x0 -> x1, Pallas kernels: none -> 37.5 us  [shards(): pl.pallas_call(functools.partial(kernel, peers, zs, scale), out_shape=(sd...]
    dot_general x29 -> x0, matrix products: 28.1 us -> none  [the longest x3 4.63 us: scatter_tiles(): jnp.einsum('tb,tnd->bnd', picker, per_tile, precision=lax.Precision.HIGHEST)]
    all_to_all x2 -> x0, starting transfers between devices: 9.45 us -> none  [the longest x1 5.3 us: shards(): lax.all_to_all(outgoing, 'nodes', split_axis=0, concat_axis=0, tiled=True)]
    unnamed x66 -> x42, local copies, waits for them, and re-layouts: 7.09 us -> 14.8 us
    gather x3 -> x0, local copies, waits for them, and re-layouts: 4.8 us -> none  [gather_tiles(): picked = table.reshape(-1, tile, table.shape[-1])[blocks]]
    mul x6 -> x0, other arithmetic: 4.32 us -> none  [the longest x5 3.99 us: shards(): scaled = [value * scale_factor for value in summed]]
  transfers between devices with their start and end apart: 3 -> 0, of which waited for: 2 -> 0; matrix products, arithmetic and copies ran while one was open for 6% -> 0% of each run, Pallas kernels for 0% -> 0%
where the time goes in v1:
time: 53.6 us; the launch traced here: 53.1 us
  Pallas kernels  37.5 us (70%)
  local copies, waits for them, and re-layouts  14.8 us (28%)
  between operations  0.73 us (1%)
    pallas_call x1, Pallas kernels, shards(): pl.pallas_call(functools.partial(kernel, peers, zs, scale), out_shape=(sd...  37.5 us
    unnamed x42, local copies, waits for them, and re-layouts  14.8 us

profile of v1, /device:TPU:0, one launch (start us, length us, event | category | flops | bytes accessed | tf_op | source)
XLA Modules:
  0.0 53.1 jit_solution(18349782749439134171)
XLA Ops:
  0.6 0.0 copy-start.14
  0.7 0.0 copy-start.13
  0.7 0.0 copy-start.8
  0.7 0.0 copy-start.7
  0.7 0.6 %copy-done.14 = s32[1,1,8,2]{2,3,1,0:T(2,128)S(1)} copy-done((s32[1,1,8,2]{2,3,1,0:T(2,128)S(1)}, s32[1,1,8,2]{2,3,1,0:T(2,128)}, u32[]{:S(2)}) %copy-start.14) | copy-done | bytes 88
  1.3 0.1 copy.26.sblk
  1.4 0.8 %copy.27.dblk = s32[1,1,8,2]{3,2,1,0:T(8,128)S(1)} copy(s32[1,1,8,2]{2,3,1,0:T(2,128)} %param.20) | data formatting | bytes 128 | tf_op args[4]
  2.2 0.0 copy-done.13
  2.2 0.0 copy-done.8
  2.2 0.0 copy-done.7
  2.2 0.0 copy-done.10
  2.2 0.0 copy-done.11
  2.2 0.0 copy-start
  2.3 1.0 %copy-done = bf16[1,2048,128]{2,1,0:T(8,128)(2,1)S(1)} copy-done((bf16[1,2048,128]{2,1,0:T(8,128)(2,1)S(1)}, bf16[1,2048,128]{2,1,0:T(8,128)(2,1)}, u32[]{:S(2)}) %copy-start) | copy-done | bytes 524312
  3.3 1.0 %copy-done.1 = bf16[1,1,8,2,128,128]{5,4,3,2,1,0:T(8,128)(2,1)S(1)} copy-done((bf16[1,1,8,2,128,128]{5,4,3,2,1,0:T(8,128)(2,1)S(1)}, bf16[1,1,8,2,128,128]{5,4,3,2,1,0:T(8,128)(2,1)}, u32[]{:S(2)}) %copy-start.1) | copy-done | bytes 524312
  4.3 1.0 %copy-done.2 = bf16[1,2048,128]{2,1,0:T(8,128)(2,1)S(1)} copy-done((bf16[1,2048,128]{2,1,0:T(8,128)(2,1)S(1)}, bf16[1,2048,128]{2,1,0:T(8,128)(2,1)}, u32[]{:S(2)}) %copy-start.2) | copy-done | bytes 524312
  5.4 0.9 %copy-done.3 = bf16[384,128]{1,0:T(8,128)(2,1)S(1)} copy-done((bf16[384,128]{1,0:T(8,128)(2,1)S(1)}, bf16[384,128]{1,0:T(8,128)(2,1)}, u32[]{:S(2)}) %copy-start.3) | copy-done | bytes 98328
  6.3 0.8 %copy-done.4 = bf16[256,128]{1,0:T(8,128)(2,1)S(1)} copy-done((bf16[256,128]{1,0:T(8,128)(2,1)S(1)}, bf16[256,128]{1,0:T(8,128)(2,1)}, u32[]{:S(2)}) %copy-start.4) | copy-done | bytes 65560
  7.1 0.8 %copy-done.5 = bf16[128,128]{1,0:T(8,128)(2,1)S(1)} copy-done((bf16[128,128]{1,0:T(8,128)(2,1)S(1)}, bf16[128,128]{1,0:T(8,128)(2,1)}, u32[]{:S(2)}) %copy-start.5) | copy-done | bytes 32792
  7.9 0.8 %copy-done.6 = bf16[128,128]{1,0:T(8,128)(2,1)S(1)} copy-done((bf16[128,128]{1,0:T(8,128)(2,1)S(1)}, bf16[128,128]{1,0:T(8,128)(2,1)}, u32[]{:S(2)}) %copy-start.6) | copy-done | bytes 32792
  8.6 0.7 %copy-done.9 = s32[1,8,8]{2,1,0:T(8,128)S(1)} copy-done((s32[1,8,8]{2,1,0:T(8,128)S(1)}, s32[1,8,8]{2,1,0:T(8,128)}, u32[]{:S(2)}) %copy-start.9) | copy-done | bytes 280
  9.3 37.5 %shard_map.231 = (bf16[1,2048,128]{2,1,0:T(8,128)(2,1)S(1)}, bf16[1,2048,128]{2,1,0:T(8,128)(2,1)S(1)}, f32[384,128]{1,0:T(8,128)S(1)}, f32[1,128]{1,0:T(1,128)S...) custom-call(bf16[1,16,128,128]{3,2,1,0:T(8,128)(2,1)S(1)} %bitcast.9, ...), custom_call_target="tpu_custom_call" | custom-call | tf_op jit(solution)/shard_map/pallas_call | solution.py:454
  46.8 0.8 %copy.38 = bf16[1,2048,128]{2,1,0:T(8,128)(2,1)} copy(bf16[1,2048,128]{2,1,0:T(8,128)(2,1)S(1)} %get-tuple-element.40) | data formatting | bytes 1048576
  47.6 0.8 %copy.39 = bf16[1,2048,128]{2,1,0:T(8,128)(2,1)} copy(bf16[1,2048,128]{2,1,0:T(8,128)(2,1)S(1)} %get-tuple-element.41) | data formatting | bytes 1048576
  48.4 0.7 %copy.40 = f32[384,128]{1,0:T(8,128)} copy(f32[384,128]{1,0:T(8,128)S(1)} %get-tuple-element.42) | data formatting | bytes 393216
  49.1 0.5 copy.41
  49.6 0.6 %copy.42 = f32[128,128]{1,0:T(8,128)} copy(f32[128,128]{1,0:T(8,128)S(1)} %get-tuple-element.44) | data formatting | bytes 131072
  50.2 0.5 copy.43
  50.7 0.7 %copy.44 = f32[256,128]{1,0:T(8,128)} copy(f32[256,128]{1,0:T(8,128)S(1)} %get-tuple-element.46) | data formatting | bytes 262144
  51.4 0.5 copy.45
  51.9 0.6 %copy.46 = f32[128,128]{1,0:T(8,128)} copy(f32[128,128]{1,0:T(8,128)S(1)} %get-tuple-element.48) | data formatting | bytes 131072
  52.5 0.5 copy.47
  (11 shorter events, 0.0 us)
Async XLA Ops:
  0.6 0.7 %copy-start.14 = (s32[1,1,8,2]{2,3,1,0:T(2,128)S(1)}, s32[1,1,8,2]{2,3,1,0:T(2,128)}, u32[]{:S(2)}) copy-start(s32[1,1,8,2]{2,3,1,0:T(2,128)} %param.18) | copy-start | bytes 196
  0.7 1.6 %copy-start.13 = (f32[128]{0:T(128)S(1)}, f32[128]{0:T(128)}, u32[]{:S(2)}) copy-start(f32[128]{0:T(128)} %param.30) | copy-start | bytes 1540
  0.7 1.5 %copy-start.8 = (s32[1,1,8,2,128]{4,3,2,1,0:T(2,128)S(1)}, s32[1,1,8,2,128]{4,3,2,1,0:T(2,128)}, u32[]{:S(2)}) copy-start(s32[1,1,8,2,128]{4,3,2,1,0:T(2,128)} %doff.1) | copy-start | bytes 24580
  0.7 1.5 %copy-start.7 = (s32[1,1,8,2,128]{4,3,2,1,0:T(2,128)S(1)}, s32[1,1,8,2,128]{4,3,2,1,0:T(2,128)}, u32[]{:S(2)}) copy-start(s32[1,1,8,2,128]{4,3,2,1,0:T(2,128)} %soff.1) | copy-start | bytes 24580
  1.4 0.8 %copy-start.10 = (f32[128]{0:T(128)S(1)}, f32[128]{0:T(128)}, u32[]{:S(2)}) copy-start(f32[128]{0:T(128)} %param.24) | copy-start | bytes 1540
  1.4 0.8 %copy-start.11 = (f32[128]{0:T(128)S(1)}, f32[128]{0:T(128)}, u32[]{:S(2)}) copy-start(f32[128]{0:T(128)} %param.26) | copy-start | bytes 1540
  1.4 0.8 %copy-start.12 = (f32[128]{0:T(128)S(1)}, f32[128]{0:T(128)}, u32[]{:S(2)}) copy-start(f32[128]{0:T(128)} %param.28) | copy-start | bytes 1540
  2.2 1.0 %copy-start = (bf16[1,2048,128]{2,1,0:T(8,128)(2,1)S(1)}, bf16[1,2048,128]{2,1,0:T(8,128)(2,1)}, u32[]{:S(2)}) copy-start(bf16[1,2048,128]{2,1,0:T(8,128)(2,1)} %param.16) | copy-start | bytes 1572868
  3.3 1.0 %copy-start.1 = (bf16[1,1,8,2,128,128]{5,4,3,2,1,0:T(8,128)(2,1)S(1)}, bf16[1,1,8,2,128,128]{5,4,3,2,1,0:T(8,128)(2,1)}, u32[]{:S(2)}) copy-start(bf16[1,1,8,2,128,128]{5,4,3,2,1,0:T(8,128)(2,1)} %lat.1) | copy-start | bytes 1572868
  4.3 1.0 %copy-start.2 = (bf16[1,2048,128]{2,1,0:T(8,128)(2,1)S(1)}, bf16[1,2048,128]{2,1,0:T(8,128)(2,1)}, u32[]{:S(2)}) copy-start(bf16[1,2048,128]{2,1,0:T(8,128)(2,1)} %cot.1) | copy-start | bytes 1572868
  5.4 0.9 %copy-start.3 = (bf16[384,128]{1,0:T(8,128)(2,1)S(1)}, bf16[384,128]{1,0:T(8,128)(2,1)}, u32[]{:S(2)}) copy-start(bf16[384,128]{1,0:T(8,128)(2,1)} %w1.1) | copy-start | bytes 294916
  6.3 0.8 %copy-start.4 = (bf16[256,128]{1,0:T(8,128)(2,1)S(1)}, bf16[256,128]{1,0:T(8,128)(2,1)}, u32[]{:S(2)}) copy-start(bf16[256,128]{1,0:T(8,128)(2,1)} %wn1.1) | copy-start | bytes 196612
  7.1 0.8 %copy-start.5 = (bf16[128,128]{1,0:T(8,128)(2,1)S(1)}, bf16[128,128]{1,0:T(8,128)(2,1)}, u32[]{:S(2)}) copy-start(bf16[128,128]{1,0:T(8,128)(2,1)} %w2.1) | copy-start | bytes 98308
  7.9 0.8 %copy-start.6 = (bf16[128,128]{1,0:T(8,128)(2,1)S(1)}, bf16[128,128]{1,0:T(8,128)(2,1)}, u32[]{:S(2)}) copy-start(bf16[128,128]{1,0:T(8,128)(2,1)} %wn2.1) | copy-start | bytes 98308
  8.6 0.7 %copy-start.9 = (s32[1,8,8]{2,1,0:T(8,128)S(1)}, s32[1,8,8]{2,1,0:T(8,128)}, u32[]{:S(2)}) copy-start(s32[1,8,8]{2,1,0:T(8,128)} %cnt.1) | copy-start | bytes 772

commit v2 on v1

--- a/solution.py
+++ b/solution.py
@@ -29,10 +29,23 @@
     return v * s, s * (1.0 + v * (1.0 - s))
 
 
+def staged(peers, zs, scale, held, *refs):
+    ins, rest = list(refs[:16]), list(refs[16:])
+    sems = rest.pop()
+    local, rest = rest[-len(held) :], rest[: -len(held)]
+    copies = {}
+    for n, j in enumerate(held):
+        copies[j] = pltpu.make_async_copy(ins[j], local[n], sems.at[n])
+        copies[j].start()
+        ins[j] = local[n]
+    kernel(peers, zs, scale, copies, *ins, *rest)
+
+
 def kernel(
     peers,
     zs,
     scale,
+    copies,
     nodes,
     lat,
     sblk,
@@ -136,6 +149,8 @@
             block = nodes[0, sblk[0, 0, p, k]]
             into[p, k] = dot_tl(hot, block).astype(BF16)
 
+    for j in (0, 3):
+        copies[j].wait()
     gather_src(me, rh)
     pl.semaphore_wait(barrier, peers - 1 + zs - 1)
 
@@ -149,6 +164,10 @@
         return c
 
     lax.fori_loop(1, peers, send_a, 0)
+
+    for j in copies:
+        if j not in (0, 3):
+            copies[j].wait()
 
     def local(s, c):
         h = []
@@ -166,7 +185,7 @@
         slope[s] = z.reshape(slots, tile, width)
         return c
 
-    lax.fori_loop(0, peers, local, 0)
+    lax.fori_loop(0, peers, local, 0, unroll=4)
 
     cw[...] = dot_tr(cot[0], wn2[...])
 
@@ -314,7 +333,7 @@
             st[s, k] = dot(pd[s, k], g1[s, k])
         return c
 
-    lax.fori_loop(0, peers, tiles_d, 0)
+    lax.fori_loop(0, peers, tiles_d, 0, unroll=4)
 
     def spread_d(b, c):
         sd[pl.ds(pl.multiple_of(b * tile, tile), tile), :] = spread(st, dblk, b).astype(BF16)
@@ -447,57 +466,12 @@
     chunk = -(-need // (16 * peers)) * 16
     vec = lambda v: v.reshape(1, -1)
     vm = pl.BlockSpec(memory_space=pltpu.VMEM)
+    hbm = pl.BlockSpec(memory_space=pl.ANY)
     sm = pl.BlockSpec(memory_space=pltpu.SMEM)
     tiles = (peers, slots, tile, width)
     sds = jax.ShapeDtypeStruct
     dma = pltpu.SemaphoreType.DMA
-    outs = pl.pallas_call(
-        functools.partial(kernel, peers, zs, scale),
-        out_shape=(
-            sds((1, rows, width), BF16),
-            sds((1, rows, width), BF16),
-            sds((3 * width, width), F32),
-            sds((1, width), F32),
-            sds((width, width), F32),
-            sds((1, width), F32),
-            sds((2 * width, width), F32),
-            sds((1, width), F32),
-            sds((width, width), F32),
-            sds((1, width), F32),
-        ),
-        in_specs=[vm, vm, sm, vm, sm, vm, sm] + [vm] * 9,
-        out_specs=(vm,) * 10,
-        scratch_shapes=[
-            pltpu.VMEM(tiles, BF16),
-            pltpu.VMEM(tiles, BF16),
-            pltpu.VMEM((peers, slots, tile, tile), BF16),
-            pltpu.VMEM((peers, slots, tile, tile), BF16),
-            pltpu.VMEM(tiles, BF16),
-            pltpu.VMEM(tiles, F32),
-            pltpu.VMEM(tiles, BF16),
-            pltpu.VMEM(tiles, BF16),
-            pltpu.VMEM(tiles, BF16),
-            pltpu.VMEM(tiles, BF16),
-            pltpu.VMEM(tiles, F32),
-            pltpu.VMEM(tiles, F32),
-            pltpu.VMEM((rows, width), F32),
-            pltpu.VMEM((rows, width), BF16),
-            pltpu.VMEM((rows, width), BF16),
-            pltpu.VMEM((rows, width), BF16),
-            pltpu.VMEM((rows // tile, tile, width), BF16),
-            pltpu.VMEM((rows, width), BF16),
-            pltpu.VMEM((peers * chunk, width), BF16),
-            pltpu.VMEM((peers, chunk, width), BF16),
-            pltpu.VMEM((zs, chunk, width), BF16),
-            pltpu.VMEM((peers, chunk, width), BF16),
-        ]
-        + [dma((peers,))] * 6
-        + [dma((zs,))] * 2
-        + [dma((peers,))] * 2,
-        compiler_params=pltpu.CompilerParams(
-            collective_id=0, has_side_effects=True, vmem_limit_bytes=48 * 1024 * 1024
-        ),
-    )(
+    args = (
         nodes_in.reshape(1, rows // tile, tile, width),
         edge_latents,
         src_block,
@@ -515,6 +489,56 @@
         vec(b_node2),
         cotangent,
     )
+    held = (3, 0, 5, 1, 7, 8, 15, 9, 10, 11, 12, 13, 14)
+    outs = pl.pallas_call(
+        functools.partial(staged, peers, zs, scale, held),
+        out_shape=(
+            sds((1, rows, width), BF16),
+            sds((1, rows, width), BF16),
+            sds((3 * width, width), F32),
+            sds((1, width), F32),
+            sds((width, width), F32),
+            sds((1, width), F32),
+            sds((2 * width, width), F32),
+            sds((1, width), F32),
+            sds((width, width), F32),
+            sds((1, width), F32),
+        ),
+        in_specs=[sm if j in (2, 4, 6) else hbm for j in range(16)],
+        out_specs=(vm,) * 10,
+        scratch_shapes=[
+            pltpu.VMEM(tiles, BF16),
+            pltpu.VMEM(tiles, BF16),
+            pltpu.VMEM((peers, slots, tile, tile), BF16),
+            pltpu.VMEM((peers, slots, tile, tile), BF16),
+            pltpu.VMEM(tiles, BF16),
+            pltpu.VMEM(tiles, F32),
+            pltpu.VMEM(tiles, BF16),
+            pltpu.VMEM(tiles, BF16),
+            pltpu.VMEM(tiles, BF16),
+            pltpu.VMEM(tiles, BF16),
+            pltpu.VMEM(tiles, F32),
+            pltpu.VMEM(tiles, F32),
+            pltpu.VMEM((rows, width), F32),
+            pltpu.VMEM((rows, width), BF16),
+            pltpu.VMEM((rows, width), BF16),
+            pltpu.VMEM((rows, width), BF16),
+            pltpu.VMEM((rows // tile, tile, width), BF16),
+            pltpu.VMEM((rows, width), BF16),
+            pltpu.VMEM((peers * chunk, width), BF16),
+            pltpu.VMEM((peers, chunk, width), BF16),
+            pltpu.VMEM((zs, chunk, width), BF16),
+            pltpu.VMEM((peers, chunk, width), BF16),
+        ]
+        + [dma((peers,))] * 6
+        + [dma((zs,))] * 2
+        + [dma((peers,))] * 2
+        + [pltpu.VMEM(args[j].shape, args[j].dtype) for j in held]
+        + [dma((len(held),))],
+        compiler_params=pltpu.CompilerParams(
+            collective_id=0, has_side_effects=True, vmem_limit_bytes=56 * 1024 * 1024
+        ),
+    )(*args)
     outs = list(outs)
     for j in (3, 5, 7, 9):
         outs[j] = outs[j].reshape(-1)

time: 53.6 us -> 49.7 us (0.927)
  local copies, waits for them, and re-layouts: 14.8 us -> 9.76 us
  Pallas kernels: 37.5 us -> 38.9 us
    unnamed x42 -> x34, local copies, waits for them, and re-layouts: 14.8 us -> 9.76 us
    pallas_call x1, Pallas kernels: 37.5 us -> 38.9 us  [shards(): pl.pallas_call(functools.partial(staged, peers, zs, scale, held), out_sha...]
where the time goes in v2:
time: 49.7 us; the launch traced here: 49.4 us
  Pallas kernels  38.9 us (78%)
  local copies, waits for them, and re-layouts  9.76 us (20%)
  between operations  0.68 us (1%)
    pallas_call x1, Pallas kernels, shards(): pl.pallas_call(functools.partial(staged, peers, zs, scale, held), out_sha...  38.9 us
    unnamed x34, local copies, waits for them, and re-layouts  9.76 us

profile of v2, /device:TPU:0, one launch (start us, length us, event | category | flops | bytes accessed | tf_op | source)
XLA Modules:
  0.0 49.4 jit_solution(10323543673011434758)
XLA Ops:
  0.6 0.0 copy-start.5
  0.7 0.7 %copy-done.5 = s32[1,1,8,2]{2,3,1,0:T(2,128)S(1)} copy-done((s32[1,1,8,2]{2,3,1,0:T(2,128)S(1)}, s32[1,1,8,2]{2,3,1,0:T(2,128)}, u32[]{:S(2)}) %copy-start.5) | copy-done | bytes 88
  1.3 0.0 copy-start.6
  1.3 0.7 %copy.26.refs_2_ = s32[1,1,8,2]{3,2,1,0:T(8,128)} copy(s32[1,1,8,2]{2,3,1,0:T(2,128)S(1)} %copy-done.5) | data formatting | bytes 128 | tf_op args[2]
  2.0 0.0 copy-done.6
  2.0 0.7 %copy.27.refs_4_ = s32[1,1,8,2]{3,2,1,0:T(8,128)} copy(s32[1,1,8,2]{2,3,1,0:T(2,128)S(1)} %copy-done.6) | data formatting | bytes 128 | tf_op args[4]
  2.7 38.9 %shard_map.231 = (bf16[1,2048,128]{2,1,0:T(8,128)(2,1)}, bf16[1,2048,128]{2,1,0:T(8,128)(2,1)}, f32[384,128]{1,0:T(8,128)}, f32[1,128]{1,0:T(1,128)}, f32[128,12...) custom-call(bf16[1,16,128,128]{3,2,1,0:T(8,128)(2,1)} %bitcast.9, ...), custom_call_target="tpu_custom_call" | custom-call | tf_op jit(solution)/shard_map/pallas_call | solution.py:493
  41.6 0.0 copy-start
  41.6 1.9 %copy.38 = bf16[1,2048,128]{2,1,0:T(8,128)(2,1)} copy(bf16[1,2048,128]{2,1,0:T(8,128)(2,1)} %get-tuple-element.40) | data formatting | bytes 1048576
  43.5 0.0 copy-done
  43.5 0.0 copy-start.1
  43.5 0.8 %copy.39 = bf16[1,2048,128]{2,1,0:T(8,128)(2,1)} copy(bf16[1,2048,128]{2,1,0:T(8,128)(2,1)S(1)} %copy-done) | data formatting | bytes 1048576
  44.3 0.3 copy-done.1
  44.6 0.0 copy-start.10
  44.6 0.0 copy-start.4
  44.7 0.7 %copy.40 = f32[384,128]{1,0:T(8,128)} copy(f32[384,128]{1,0:T(8,128)S(1)} %copy-done.1) | data formatting | bytes 393216
  45.3 0.0 copy-done.10
  45.3 0.0 copy-start.2
  45.3 0.5 %copy.41 = f32[128]{0:T(128)} copy(f32[128]{0:T(128)S(1)} %bitcast.17) | data formatting | bytes 1024
  45.8 0.0 copy-done.4
  45.8 0.0 copy-start.9
  45.8 0.6 %copy.42 = f32[128,128]{1,0:T(8,128)} copy(f32[128,128]{1,0:T(8,128)S(1)} %copy-done.4) | data formatting | bytes 131072
  46.5 0.0 copy-done.9
  46.5 0.5 %copy.43 = f32[128]{0:T(128)} copy(f32[128]{0:T(128)S(1)} %bitcast.16) | data formatting | bytes 1024
  47.0 0.0 copy-done.2
  47.0 0.7 %copy.44 = f32[256,128]{1,0:T(8,128)} copy(f32[256,128]{1,0:T(8,128)S(1)} %copy-done.2) | data formatting | bytes 262144
  47.7 0.0 copy-done.8
  47.7 0.5 %copy.45 = f32[128]{0:T(128)} copy(f32[128]{0:T(128)S(1)} %bitcast.15) | data formatting | bytes 1024
  48.2 0.0 copy-done.3
  48.2 0.6 %copy.46 = f32[128,128]{1,0:T(8,128)} copy(f32[128,128]{1,0:T(8,128)S(1)} %copy-done.3) | data formatting | bytes 131072
  48.8 0.0 copy-done.7
  48.8 0.5 %copy.47 = f32[128]{0:T(128)} copy(f32[128]{0:T(128)S(1)} %bitcast.14) | data formatting | bytes 1024
  (3 shorter events, 0.0 us)
Async XLA Ops:
  0.6 0.7 %copy-start.5 = (s32[1,1,8,2]{2,3,1,0:T(2,128)S(1)}, s32[1,1,8,2]{2,3,1,0:T(2,128)}, u32[]{:S(2)}) copy-start(s32[1,1,8,2]{2,3,1,0:T(2,128)} %param.18) | copy-start | bytes 196
  1.3 0.7 %copy-start.6 = (s32[1,1,8,2]{2,3,1,0:T(2,128)S(1)}, s32[1,1,8,2]{2,3,1,0:T(2,128)}, u32[]{:S(2)}) copy-start(s32[1,1,8,2]{2,3,1,0:T(2,128)} %param.20) | copy-start | bytes 196
  41.6 1.9 %copy-start = (bf16[1,2048,128]{2,1,0:T(8,128)(2,1)S(1)}, bf16[1,2048,128]{2,1,0:T(8,128)(2,1)}, u32[]{:S(2)}) copy-start(bf16[1,2048,128]{2,1,0:T(8,128)(2,1)} %get-tuple-element.41) | copy-start | bytes 1572868
  43.5 1.1 %copy-start.1 = (f32[384,128]{1,0:T(8,128)S(1)}, f32[384,128]{1,0:T(8,128)}, u32[]{:S(2)}) copy-start(f32[384,128]{1,0:T(8,128)} %get-tuple-element.42) | copy-start | bytes 589828
  44.6 0.7 %copy-start.10 = (f32[1,128]{1,0:T(1,128)S(1)}, f32[1,128]{1,0:T(1,128)}, u32[]{:S(2)}) copy-start(f32[1,128]{1,0:T(1,128)} %get-tuple-element.23) | copy-start | bytes 1540
  44.6 1.2 %copy-start.4 = (f32[128,128]{1,0:T(8,128)S(1)}, f32[128,128]{1,0:T(8,128)}, u32[]{:S(2)}) copy-start(f32[128,128]{1,0:T(8,128)} %get-tuple-element.44) | copy-start | bytes 196612
  45.3 1.7 %copy-start.2 = (f32[256,128]{1,0:T(8,128)S(1)}, f32[256,128]{1,0:T(8,128)}, u32[]{:S(2)}) copy-start(f32[256,128]{1,0:T(8,128)} %get-tuple-element.46) | copy-start | bytes 393220
  45.8 0.7 %copy-start.9 = (f32[1,128]{1,0:T(1,128)S(1)}, f32[1,128]{1,0:T(1,128)}, u32[]{:S(2)}) copy-start(f32[1,128]{1,0:T(1,128)} %get-tuple-element.25) | copy-start | bytes 1540
  47.0 0.7 %copy-start.8 = (f32[1,128]{1,0:T(1,128)S(1)}, f32[1,128]{1,0:T(1,128)}, u32[]{:S(2)}) copy-start(f32[1,128]{1,0:T(1,128)} %get-tuple-element.27) | copy-start | bytes 1540
  47.0 1.2 %copy-start.3 = (f32[128,128]{1,0:T(8,128)S(1)}, f32[128,128]{1,0:T(8,128)}, u32[]{:S(2)}) copy-start(f32[128,128]{1,0:T(8,128)} %get-tuple-element.48) | copy-start | bytes 196612
  48.2 0.6 %copy-start.7 = (f32[1,128]{1,0:T(1,128)S(1)}, f32[1,128]{1,0:T(1,128)}, u32[]{:S(2)}) copy-start(f32[1,128]{1,0:T(1,128)} %get-tuple-element.29) | copy-start | bytes 1540

commit v3 on v2

--- a/solution.py
+++ b/solution.py
@@ -64,14 +64,7 @@
     cot,
     upd,
     ngrad,
-    gw1,
-    gb1,
-    gw2,
-    gb2,
-    gwn1,
-    gbn1,
-    gwn2,
-    gbn2,
+    grads,
     hs,
     rh,
     ps,
@@ -220,7 +213,7 @@
             0, peers, body, jnp.zeros((tile, width), F32), unroll=True if peers <= 8 else 8
         )
 
-    group = 4 if nblk % 4 == 0 else 1
+    group = 8 if nblk % 8 == 0 else 1
     span = group * tile
 
     def node(c, carry):
@@ -411,16 +404,7 @@
         return c
 
     lax.fori_loop(1, peers, recv_g, 0)
-    full = abuf[...].reshape(peers * chunk, width)
-    gw1[...] = full[: 3 * width].astype(F32)
-    gw2[...] = full[3 * width : 4 * width].astype(F32)
-    gwn1[...] = full[4 * width : 6 * width].astype(F32)
-    gwn2[...] = full[6 * width : 7 * width].astype(F32)
-    last = full[7 * width : 7 * width + 16].astype(F32)
-    gb1[...] = last[0:1]
-    gb2[...] = last[1:2]
-    gbn1[...] = last[2:3]
-    gbn2[...] = last[3:4]
+    grads[...] = abuf[...].reshape(peers * chunk, width)
 
     def drain(i, c):
         p = lax.rem(me + i, peers)
@@ -495,17 +479,10 @@
         out_shape=(
             sds((1, rows, width), BF16),
             sds((1, rows, width), BF16),
-            sds((3 * width, width), F32),
-            sds((1, width), F32),
-            sds((width, width), F32),
-            sds((1, width), F32),
-            sds((2 * width, width), F32),
-            sds((1, width), F32),
-            sds((width, width), F32),
-            sds((1, width), F32),
+            sds((peers * chunk, width), BF16),
         ),
         in_specs=[sm if j in (2, 4, 6) else hbm for j in range(16)],
-        out_specs=(vm,) * 10,
+        out_specs=(vm,) * 3,
         scratch_shapes=[
             pltpu.VMEM(tiles, BF16),
             pltpu.VMEM(tiles, BF16),
@@ -539,10 +516,22 @@
             collective_id=0, has_side_effects=True, vmem_limit_bytes=56 * 1024 * 1024
         ),
     )(*args)
-    outs = list(outs)
-    for j in (3, 5, 7, 9):
-        outs[j] = outs[j].reshape(-1)
-    return tuple(outs)
+    upd, ngrad, grads = outs
+    grads = grads.astype(F32)
+    cut = lambda i, j: grads[i * width : j * width]
+    line = lambda i: grads[7 * width + i]
+    return (
+        upd,
+        ngrad,
+        cut(0, 3),
+        line(0),
+        cut(3, 4),
+        line(1),
+        cut(4, 6),
+        line(2),
+        cut(6, 7),
+        line(3),
+    )
 
 
 def solution(mesh):

time: 49.7 us -> 47.1 us (0.948)
  local copies, waits for them, and re-layouts: 9.76 us -> 6.6 us
  other arithmetic: 0 us -> 1.05 us
    unnamed x34 -> x12, local copies, waits for them, and re-layouts: 9.76 us -> 4.06 us
    slice x0 -> x3, local copies, waits for them, and re-layouts: none -> 2.01 us  [shards(): cut = lambda i, j: grads[i * width:j * width]]
    convert_element_type x0 -> x1, other arithmetic: none -> 1.05 us  [shards(): grads = grads.astype(F32)]
    squeeze x0 -> x1, local copies, waits for them, and re-layouts: none -> 0.53 us  [shards(): line = lambda i: grads[7 * width + i]]
where the time goes in v3:
time: 47.1 us; the launch traced here: 46.8 us
  Pallas kernels  38.5 us (82%)
  local copies, waits for them, and re-layouts  6.6 us (14%)
  other arithmetic  1.05 us (2%)
  between operations  0.68 us (1%)
    pallas_call x1, Pallas kernels, shards(): pl.pallas_call(functools.partial(staged, peers, zs, scale, held), out_sha...  38.5 us
    unnamed x12, local copies, waits for them, and re-layouts  4.06 us
    slice x3, local copies, waits for them, and re-layouts, shards(): cut = lambda i, j: grads[i * width:j * width]  2.01 us
    convert_element_type x1, other arithmetic, shards(): grads = grads.astype(F32)  1.05 us

profile of v3, /device:TPU:0, one launch (start us, length us, event | category | flops | bytes accessed | tf_op | source)
XLA Modules:
  0.0 46.8 jit_solution(72777096782153533)
XLA Ops:
  0.6 0.0 copy-start.3
  0.7 1.4 %copy.26.refs_2_ = s32[1,1,8,2]{3,2,1,0:T(8,128)} copy(s32[1,1,8,2]{2,3,1,0:T(2,128)} %param.18) | data formatting | bytes 128 | tf_op args[2]
  2.0 0.0 copy-done.3
  2.0 0.7 %copy.27.refs_4_ = s32[1,1,8,2]{3,2,1,0:T(8,128)} copy(s32[1,1,8,2]{2,3,1,0:T(2,128)S(1)} %copy-done.3) | data formatting | bytes 128 | tf_op args[4]
  2.7 38.5 %shard_map.231 = (bf16[1,2048,128]{2,1,0:T(8,128)(2,1)}, bf16[1,2048,128]{2,1,0:T(8,128)(2,1)}, bf16[1024,128]{1,0:T(8,128)(2,1)}) custom-call(bf16[1,16,128,128]{3,2,1,0:T(8,128)(2,1)} %bitcast.13, bf16[1,1,8,2,128,128]{5,4,3,2,1,0:T(8,128)(2,1)} %refs_1_.1, s32[1,1,8,2]{3,2,1,0:T(8,128)} %copy.26.refs_2_, s32[1,1,8,2,128]{4,3,2,1,0:T(2,128)} %refs_3_.1, ...), custom_call_target="tpu_custom_call" | custom-call | tf_op jit(solution)/shard_map/pallas_call | solution.py:477
  41.2 0.0 copy-start
  41.2 1.1 %convert_element_type.3 = f32[1024,128]{1,0:T(8,128)S(1)} convert(bf16[1024,128]{1,0:T(8,128)(2,1)} %get-tuple-element.15) | non-fusion elementwise | flops 131072 | bytes 786432 | tf_op jit(solution)/shard_map/convert_element_type | solution.py:520
  42.2 0.0 copy-start.2
  42.2 0.5 %slice_bitcast_fusion = (f32[128]{0:T(128)}, f32[128]{0:T(128)}, f32[128]{0:T(128)}, f32[128]{0:T(128)}) fusion(f32[1024,128]{1,0:T(8,128)S(1)} %convert_element_type.3), kind=kLoop, calls=%fused_computation | loop fusion | bytes 4096 | tf_op jit(solution)/shard_map/squeeze | solution.py:522
  42.8 0.0 copy-done
  42.8 0.7 %fusion = (f32[128,128]{1,0:T(8,128)}, f32[128,128]{1,0:T(8,128)}) fusion(bf16[1024,128]{1,0:T(8,128)(2,1)S(1)} %copy-done), kind=kLoop, calls=%fused_computation.4 | loop fusion | bytes 262144 | tf_op jit(solution)/shard_map/slice | solution.py:521
  43.4 0.7 %slice.32 = f32[384,128]{1,0:T(8,128)} slice(bf16[1024,128]{1,0:T(8,128)(2,1)S(1)} %copy-done), slice={[0:384], [0:128]} | slice | bytes 393216 | tf_op jit(solution)/shard_map/slice | solution.py:521
  44.1 0.7 %slice.36 = f32[256,128]{1,0:T(8,128)} slice(bf16[1024,128]{1,0:T(8,128)(2,1)S(1)} %copy-done), slice={[512:768], [0:128]} | slice | bytes 262144 | tf_op jit(solution)/shard_map/slice | solution.py:521
  44.8 0.0 copy-done.2
  44.8 0.0 copy-start.1
  44.8 0.8 %copy.30 = bf16[1,2048,128]{2,1,0:T(8,128)(2,1)} copy(bf16[1,2048,128]{2,1,0:T(8,128)(2,1)S(1)} %copy-done.2) | data formatting | bytes 1048576
  45.6 0.4 copy-done.1
  46.0 0.8 %copy.31 = bf16[1,2048,128]{2,1,0:T(8,128)(2,1)} copy(bf16[1,2048,128]{2,1,0:T(8,128)(2,1)S(1)} %copy-done.1) | data formatting | bytes 1048576
Async XLA Ops:
  0.6 1.4 %copy-start.3 = (s32[1,1,8,2]{2,3,1,0:T(2,128)S(1)}, s32[1,1,8,2]{2,3,1,0:T(2,128)}, u32[]{:S(2)}) copy-start(s32[1,1,8,2]{2,3,1,0:T(2,128)} %param.20) | copy-start | bytes 196
  41.2 1.6 %copy-start = (bf16[1024,128]{1,0:T(8,128)(2,1)S(1)}, bf16[1024,128]{1,0:T(8,128)(2,1)}, u32[]{:S(2)}) copy-start(bf16[1024,128]{1,0:T(8,128)(2,1)} %get-tuple-element.15) | copy-start | bytes 786436
  42.2 2.6 %copy-start.2 = (bf16[1,2048,128]{2,1,0:T(8,128)(2,1)S(1)}, bf16[1,2048,128]{2,1,0:T(8,128)(2,1)}, u32[]{:S(2)}) copy-start(bf16[1,2048,128]{2,1,0:T(8,128)(2,1)} %get-tuple-element.32) | copy-start | bytes 1572868
  44.8 1.2 %copy-start.1 = (bf16[1,2048,128]{2,1,0:T(8,128)(2,1)S(1)}, bf16[1,2048,128]{2,1,0:T(8,128)(2,1)}, u32[]{:S(2)}) copy-start(bf16[1,2048,128]{2,1,0:T(8,128)(2,1)} %get-tuple-element.33) | copy-start | bytes 1572868
